TPU v7x, 32 devices: a whole 2x2x4 slice. The times are simulated.
32 devices in a mesh: groups: 2 (over y), blk: 4 (over z), heads: 2 (over x), sub: 2 (over core).
Axes of the slice: x: 2, y: 2, z: 4, core: 2. Of those that a mesh axis runs over, the one named last changes fastest.
Arguments:
- queries: bfloat16 [512, 4096], P(('groups', 'blk'), ('heads', 'sub')), parts along dimension 0, may hold values from -3 to 3
- keys: bfloat16 [16384, 4096], P(('groups', 'blk'), ('heads', 'sub')), parts along dimension 0, may hold values from -3 to 3
- values: bfloat16 [16384, 4096], P(('groups', 'blk'), ('heads', 'sub')), parts along dimension 0, may hold values from -6 to 6
- out_weight: bfloat16 [4096, 4096], P(('heads', 'sub')), may hold values from -0.125 to 0.125
- counts: int32 [32], P('groups'), parts along dimension 0, may hold values from 1 to 16, 32 in all
- slot_of: int32 [64], P('groups'), parts along dimension 0, may hold values from 0 to 31, each once
- beam_request: int32 [512], P('groups'), parts along dimension 0, may hold values from 0 to 15, as said below
Outputs:
- mixed: bfloat16 [512, 4096], P(('groups', 'blk'), ('heads', 'sub')), parts along dimension 0
There are 2 independent parts, one for each index of `groups`. A program takes and returns all parts, laid end to end along the dimension named above; an argument that names none is the same for every part. Nothing has to cross between parts.
Inputs may be any that keep to these rules, and one draw needn't show every extreme that they name: `beam_request`: the beams of each request are 16 consecutive rows starting at a multiple of 16; each request is named by exactly 16 beams.
All inputs are finite; a program needn't handle non-finite values.
Results may differ from a plain program's by a relative error of at most 0.012.
Values may be sent and summed in bfloat16 or wider, within the bound.
A program may use at most 64 MiB of HBM per device.

v0:
```python
import jax
import jax.numpy as jnp
from jax import lax
from jax.sharding import PartitionSpec as P

HEAD_DIM = 64
PLEN = 256


floor_score = -1e30


def shifted(value, axis, steps):
    count = lax.axis_size(axis)
    pairs = [(source, (source + steps) % count) for source in range(count)]
    return lax.ppermute(value, axis, pairs)


def slot_requests(counts, slot_of):
    passage = jnp.arange(slot_of.shape[0], dtype=jnp.int32)
    ends = jnp.cumsum(counts)
    owner = jnp.sum((passage[:, None] >= ends[None, :]).astype(jnp.int32), axis=1)
    matches = (slot_of[None, :] == passage[:, None]).astype(jnp.int32)
    return jnp.sum(matches * owner[None, :], axis=1)


def partial_state(query_rows, row_request, key_heads, value_heads, key_request):
    row_count = query_rows.shape[0]
    heads_here = key_heads.shape[1]
    query_heads = query_rows.reshape(row_count, heads_here, HEAD_DIM)
    scores = jnp.einsum("rhd,khd->rhk", query_heads, key_heads, preferred_element_type=jnp.float32)
    valid = (row_request[:, None] == key_request[None, :])[:, None, :]
    scores = jnp.where(valid, scores, floor_score)
    row_max = jnp.max(scores, axis=2)
    terms = jnp.where(valid, jnp.exp(scores - row_max[:, :, None]), 0.0)
    totals = jnp.sum(terms, axis=2)
    summed = jnp.einsum(
        "rhk,khd->rhd", terms.astype(jnp.bfloat16), value_heads, preferred_element_type=jnp.float32
    )
    return (summed.reshape(row_count, heads_here * HEAD_DIM), row_max, totals)


def combine(first, second):
    summed_a, max_a, total_a = first
    summed_b, max_b, total_b = second
    largest = jnp.maximum(max_a, max_b)
    factor_a = jnp.exp(max_a - largest)
    factor_b = jnp.exp(max_b - largest)
    row_count, heads_here = max_a.shape
    summed = summed_a.reshape(row_count, heads_here, HEAD_DIM) * factor_a[:, :, None]
    summed = summed + summed_b.reshape(row_count, heads_here, HEAD_DIM) * factor_b[:, :, None]
    return (
        summed.reshape(row_count, heads_here * HEAD_DIM),
        largest,
        total_a * factor_a + total_b * factor_b,
    )


def body(queries, keys, values, out_weight, counts, slot_of, beam_request):
    row_count, features = queries.shape
    heads_here = features // HEAD_DIM
    slot_count = keys.shape[0] // PLEN
    blk_count = lax.axis_size("blk")
    position = lax.axis_index("blk")
    every_slot = slot_requests(counts, slot_of)
    local_requests = lax.dynamic_slice_in_dim(every_slot, position * slot_count, slot_count)
    key_request = jnp.repeat(local_requests, PLEN)
    key_heads = keys.reshape(keys.shape[0], heads_here, HEAD_DIM)
    value_heads = values.reshape(values.shape[0], heads_here, HEAD_DIM)
    start_state = (
        jnp.zeros((row_count, features), jnp.float32),
        jnp.full((row_count, heads_here), floor_score, jnp.float32),
        jnp.zeros((row_count, heads_here), jnp.float32),
    )

    def visit(step_index, carry):
        visitor, state = carry
        anchor = (position - step_index) % blk_count
        row_request = lax.dynamic_slice_in_dim(beam_request, anchor * row_count, row_count)
        fresh = partial_state(visitor, row_request, key_heads, value_heads, key_request)
        state = combine(state, fresh)
        visitor = shifted(visitor, "blk", 1)
        state = shifted((state[0], state[1], state[2]), "blk", 1)
        return (visitor, state)

    final_rows, final_state = lax.fori_loop(0, blk_count, visit, (queries, start_state))
    summed, row_max, totals = final_state
    attended = (summed.reshape(row_count, heads_here, HEAD_DIM) / totals[:, :, None]).reshape(
        row_count, features
    )
    attended = attended.astype(jnp.bfloat16)
    projected = jnp.dot(attended, out_weight, preferred_element_type=jnp.float32)
    return lax.psum_scatter(
        projected.astype(jnp.bfloat16), ("heads", "sub"), scatter_dimension=1, tiled=True
    )


def solution(mesh):
    return jax.shard_map(
        body,
        mesh=mesh,
        in_specs=(
            P(("groups", "blk"), ("heads", "sub")),
            P(("groups", "blk"), ("heads", "sub")),
            P(("groups", "blk"), ("heads", "sub")),
            P(("heads", "sub"), None),
            P("groups"),
            P("groups"),
            P("groups"),
        ),
        out_specs=P(("groups", "blk"), ("heads", "sub")),
        check_vma=False,
    )
```

profile of v0, /device:TPU:0, one launch (start us, length us, event | category | flops | bytes accessed | tf_op | source)
XLA Modules:
  0.0 141.9 jit_solution(10020609875961900030)
XLA Ops:
  6.5 0.7 copy.25
  7.3 0.1 reduce
  7.4 0.1 convert_reduce_fusion
  7.5 6.6 %copy.23 = bf16[2048,1024]{0,1:T(8,128)(2,1)} copy(bf16[2048,1024]{1,0:T(8,128)(2,1)} %param.10) | data formatting | bytes 8388608 | tf_op args[1]
  14.1 6.5 %copy.24 = bf16[2048,1024]{0,1:T(8,128)(2,1)} copy(bf16[2048,1024]{1,0:T(8,128)(2,1)} %param.11) | data formatting | bytes 8388608 | tf_op args[2]
  20.6 0.1 select_reduce_fusion
  20.7 0.1 dynamic_slice.13
  20.9 88.7 %while.22 = (s32[]{:T(128)}, bf16[64,1024]{1,0:T(8,128)(2,1)S(1)}, f32[64,1024]{1,0:T(8,128)S(1)}, f32[64,16]{0,1:T(8,128)S(1)}, f32[64,16]{0,1:T(8,128)S(1)}, /...) while((s32[]{:T(128)}, bf16[64,1024]{1,0:T(8,128)(2,1)S(1)}, ...), condition=%wide.region_6.7_spmd.clone, body=%wide.region_3.6_spmd.clone.sunk | while | flops 558174208 | bytes 55305492 | solution.py:86
  21.0 0.2 reshape.111
  21.2 0.1 reshape.112
  21.3 0.1 dynamic_slice.16
  21.4 0.1 broadcast_compare_fusion.2
  21.6 3.9 %fusion.36 = (f32[64,16]{0,1:T(8,128)S(1)}, f32[16,2048,64]{1,2,0:T(8,128)S(1)}) fusion(pred[64,2048]{1,0:T(8,128)(4,1)S(1)} %broadcast_compare_fusion.2, bf16[2048,16,64]{0,2,1:T(8,128)(2,1)} %get-tuple-element.412, bf16[64,16,64]{2,1,0:T(8,128)(2,1)S(1)} %reshape.111), kind=kOutput, calls=%fused_computation.3.clone.1 | convolution fusion | flops 272628736 | bytes 12849152 | tf_op jit(solution)/shard_map/while/body/eval_jaxpr/rhd,khd->rhk/dot_general | solution.py:31
  25.5 2.4 %fusion.37 = f32[64,16]{0,1:T(8,128)S(1)} fusion(f32[16,2048,64]{1,2,0:T(8,128)S(1)} %get-tuple-element.367, f32[64,16]{0,1:T(8,128)S(1)} %get-tuple-element.368, pred[64,2048]{1,0:T(8,128)(4,1)S(1)} %broadcast_compare_fusion.2), kind=kLoop, calls=%fused_computation.4.clone.1 | loop fusion | flops 8387584 | bytes 8527872 | tf_op jit(solution)/shard_map/while/body/eval_jaxpr/reduce_sum | solution.py:36
  27.9 2.3 %fusion.38 = f32[64,16,64]{2,0,1:T(8,128)S(1)} fusion(bf16[2048,16,64]{0,2,1:T(8,128)(2,1)S(1)} %copy-done.1, f32[16,2048,64]{1,2,0:T(8,128)S(1)} %get-tuple-element.367, f32[64,16]{0,1:T(8,128)S(1)} %get-tuple-element.368, pred[64,2048]{1,0:T(8,128)(4,1)S(1)} %broadcast_compare_fusion.2, f32[64,16,64]{2,1,0:T(8,128)S(1)} %reshape.112, ...), kind=kOutput, calls=%fused_computation.13.clone.1 | convolution fusion | flops 277020672 | bytes 13250560 | tf_op jit(solution)/shard_map/while/body/eval_jaxpr/rhk,khd->rhd/dot_general | solution.py:37
  30.3 0.3 copy.42
  30.6 0.2 reshape.113
  30.7 3.1 %collective-permute-start.1 = (f32[64,1024]{1,0:T(8,128)S(1)}, f32[64,1024]{1,0:T(8,128)S(1)}, u32[]{:S(2)}, u32[]{:S(2)}) collective-permute-start(f32[64,1024]{1,0:T(8,128)S(1)} %reshape.113), channel_id=1, source_target_pairs={{0,4},{4,8},{8,12},{12,0},{1,5},{5,9},{9,13},{13,1},{2,6},{6,10},{... | collective-permute-start | bytes 786440 | tf_op jit(solution)/shard_map/while/body/eval_jaxpr/ppermute | solution.py:16
  33.8 1.6 %collective-permute-start = (bf16[64,1024]{1,0:T(8,128)(2,1)S(1)}, bf16[64,1024]{1,0:T(8,128)(2,1)S(1)}, u32[]{:S(2)}, u32[]{:S(2)}) collective-permute-start(bf16[64,1024]{1,0:T(8,128)(2,1)S(1)} %copy.49), channel_id=1, source_target_pairs={{0,4},{4,8},{8,12},{12,0},{1,5},{5,9},{9,13},{13,1},{2,6},{6,10},{... | collective-permute-start | bytes 393224 | tf_op jit(solution)/shard_map/while/body/eval_jaxpr/ppermute | solution.py:16
  35.4 1.6 %collective-permute-start.2 = (f32[64,16]{0,1:T(8,128)S(1)}, f32[64,16]{0,1:T(8,128)S(1)}, u32[]{:S(2)}, u32[]{:S(2)}) collective-permute-start(f32[64,16]{0,1:T(8,128)S(1)} %get-tuple-element.371), channel_id=1, source_target_pairs={{0,4},{4,8},{8,12},{12,0},{1,5},{5,9},{9,13},{13,1},{2,6},{6,10},{... | collective-permute-start | bytes 12296 | tf_op jit(solution)/shard_map/while/body/eval_jaxpr/ppermute | solution.py:16
  37.0 8.2 %collective-permute-done.2 = f32[64,16]{0,1:T(8,128)S(1)} collective-permute-done((f32[64,16]{0,1:T(8,128)S(1)}, f32[64,16]{0,1:T(8,128)S(1)}, u32[]{:S(2)}, u32[]{:S(2)}) %collective-permute-start.2) | collective-permute-done | bytes 4128 | tf_op jit(solution)/shard_map/while/body/eval_jaxpr/ppermute | solution.py:16
  45.2 0.1 collective-permute-done.3
  45.4 0.2 reshape.111
  45.6 0.1 reshape.112
  45.8 0.1 broadcast_compare_fusion.2
  46.0 3.9 %fusion.36 = (f32[64,16]{0,1:T(8,128)S(1)}, f32[16,2048,64]{1,2,0:T(8,128)S(1)}) fusion(pred[64,2048]{1,0:T(8,128)(4,1)S(1)} %broadcast_compare_fusion.2, bf16[2048,16,64]{0,2,1:T(8,128)(2,1)} %get-tuple-element.412, bf16[64,16,64]{2,1,0:T(8,128)(2,1)S(1)} %reshape.111), kind=kOutput, calls=%fused_computation.3.clone.1 | convolution fusion | flops 272628736 | bytes 12849152 | tf_op jit(solution)/shard_map/while/body/eval_jaxpr/rhd,khd->rhk/dot_general | solution.py:31
  49.9 2.4 %fusion.37 = f32[64,16]{0,1:T(8,128)S(1)} fusion(f32[16,2048,64]{1,2,0:T(8,128)S(1)} %get-tuple-element.367, f32[64,16]{0,1:T(8,128)S(1)} %get-tuple-element.368, pred[64,2048]{1,0:T(8,128)(4,1)S(1)} %broadcast_compare_fusion.2), kind=kLoop, calls=%fused_computation.4.clone.1 | loop fusion | flops 8387584 | bytes 8527872 | tf_op jit(solution)/shard_map/while/body/eval_jaxpr/reduce_sum | solution.py:36
  52.3 2.4 %fusion.38 = f32[64,16,64]{2,0,1:T(8,128)S(1)} fusion(bf16[2048,16,64]{0,2,1:T(8,128)(2,1)S(1)} %copy-done.1, f32[16,2048,64]{1,2,0:T(8,128)S(1)} %get-tuple-element.367, f32[64,16]{0,1:T(8,128)S(1)} %get-tuple-element.368, pred[64,2048]{1,0:T(8,128)(4,1)S(1)} %broadcast_compare_fusion.2, f32[64,16,64]{2,1,0:T(8,128)S(1)} %reshape.112, ...), kind=kOutput, calls=%fused_computation.13.clone.1 | convolution fusion | flops 277020672 | bytes 13250560 | tf_op jit(solution)/shard_map/while/body/eval_jaxpr/rhk,khd->rhd/dot_general | solution.py:37
  54.7 0.3 copy.42
  55.0 0.2 reshape.113
  55.2 1.3 collective-permute-start
  56.5 1.6 %collective-permute-start.2 = (f32[64,16]{0,1:T(8,128)S(1)}, f32[64,16]{0,1:T(8,128)S(1)}, u32[]{:S(2)}, u32[]{:S(2)}) collective-permute-start(f32[64,16]{0,1:T(8,128)S(1)} %get-tuple-element.371), channel_id=1, source_target_pairs={{0,4},{4,8},{8,12},{12,0},{1,5},{5,9},{9,13},{13,1},{2,6},{6,10},{... | collective-permute-start | bytes 12296 | tf_op jit(solution)/shard_map/while/body/eval_jaxpr/ppermute | solution.py:16
  58.1 2.1 %collective-permute-start.3 = (f32[64,16]{0,1:T(8,128)S(1)}, f32[64,16]{0,1:T(8,128)S(1)}, u32[]{:S(2)}, u32[]{:S(2)}) collective-permute-start(f32[64,16]{0,1:T(8,128)S(1)} %get-tuple-element.372), channel_id=1, source_target_pairs={{0,4},{4,8},{8,12},{12,0},{1,5},{5,9},{9,13},{13,1},{2,6},{6,10},{... | collective-permute-start | bytes 12296 | tf_op jit(solution)/shard_map/while/body/eval_jaxpr/ppermute | solution.py:16
  60.2 7.4 %collective-permute-done.2 = f32[64,16]{0,1:T(8,128)S(1)} collective-permute-done((f32[64,16]{0,1:T(8,128)S(1)}, f32[64,16]{0,1:T(8,128)S(1)}, u32[]{:S(2)}, u32[]{:S(2)}) %collective-permute-start.2) | collective-permute-done | bytes 4128 | tf_op jit(solution)/shard_map/while/body/eval_jaxpr/ppermute | solution.py:16
  67.6 0.1 collective-permute-done.3
  67.8 0.2 reshape.111
  67.9 0.1 reshape.112
  68.2 0.1 broadcast_compare_fusion.2
  68.3 3.9 %fusion.36 = (f32[64,16]{0,1:T(8,128)S(1)}, f32[16,2048,64]{1,2,0:T(8,128)S(1)}) fusion(pred[64,2048]{1,0:T(8,128)(4,1)S(1)} %broadcast_compare_fusion.2, bf16[2048,16,64]{0,2,1:T(8,128)(2,1)} %get-tuple-element.412, bf16[64,16,64]{2,1,0:T(8,128)(2,1)S(1)} %reshape.111), kind=kOutput, calls=%fused_computation.3.clone.1 | convolution fusion | flops 272628736 | bytes 12849152 | tf_op jit(solution)/shard_map/while/body/eval_jaxpr/rhd,khd->rhk/dot_general | solution.py:31
  72.2 2.4 %fusion.37 = f32[64,16]{0,1:T(8,128)S(1)} fusion(f32[16,2048,64]{1,2,0:T(8,128)S(1)} %get-tuple-element.367, f32[64,16]{0,1:T(8,128)S(1)} %get-tuple-element.368, pred[64,2048]{1,0:T(8,128)(4,1)S(1)} %broadcast_compare_fusion.2), kind=kLoop, calls=%fused_computation.4.clone.1 | loop fusion | flops 8387584 | bytes 8527872 | tf_op jit(solution)/shard_map/while/body/eval_jaxpr/reduce_sum | solution.py:36
  74.7 2.4 %fusion.38 = f32[64,16,64]{2,0,1:T(8,128)S(1)} fusion(bf16[2048,16,64]{0,2,1:T(8,128)(2,1)S(1)} %copy-done.1, f32[16,2048,64]{1,2,0:T(8,128)S(1)} %get-tuple-element.367, f32[64,16]{0,1:T(8,128)S(1)} %get-tuple-element.368, pred[64,2048]{1,0:T(8,128)(4,1)S(1)} %broadcast_compare_fusion.2, f32[64,16,64]{2,1,0:T(8,128)S(1)} %reshape.112, ...), kind=kOutput, calls=%fused_computation.13.clone.1 | convolution fusion | flops 277020672 | bytes 13250560 | tf_op jit(solution)/shard_map/while/body/eval_jaxpr/rhk,khd->rhd/dot_general | solution.py:37
  77.0 0.3 copy.42
  77.3 0.2 reshape.113
  77.6 0.7 collective-permute-start.2
  78.3 4.2 %collective-permute-start.3 = (f32[64,16]{0,1:T(8,128)S(1)}, f32[64,16]{0,1:T(8,128)S(1)}, u32[]{:S(2)}, u32[]{:S(2)}) collective-permute-start(f32[64,16]{0,1:T(8,128)S(1)} %get-tuple-element.372), channel_id=1, source_target_pairs={{0,4},{4,8},{8,12},{12,0},{1,5},{5,9},{9,13},{13,1},{2,6},{6,10},{... | collective-permute-start | bytes 12296 | tf_op jit(solution)/shard_map/while/body/eval_jaxpr/ppermute | solution.py:16
  82.5 6.5 %collective-permute-done.2 = f32[64,16]{0,1:T(8,128)S(1)} collective-permute-done((f32[64,16]{0,1:T(8,128)S(1)}, f32[64,16]{0,1:T(8,128)S(1)}, u32[]{:S(2)}, u32[]{:S(2)}) %collective-permute-start.2) | collective-permute-done | bytes 4128 | tf_op jit(solution)/shard_map/while/body/eval_jaxpr/ppermute | solution.py:16
  89.0 0.1 collective-permute-done.3
  89.2 0.2 reshape.111
  89.4 0.1 reshape.112
  89.6 0.1 broadcast_compare_fusion.2
  89.8 3.9 %fusion.36 = (f32[64,16]{0,1:T(8,128)S(1)}, f32[16,2048,64]{1,2,0:T(8,128)S(1)}) fusion(pred[64,2048]{1,0:T(8,128)(4,1)S(1)} %broadcast_compare_fusion.2, bf16[2048,16,64]{0,2,1:T(8,128)(2,1)} %get-tuple-element.412, bf16[64,16,64]{2,1,0:T(8,128)(2,1)S(1)} %reshape.111), kind=kOutput, calls=%fused_computation.3.clone.1 | convolution fusion | flops 272628736 | bytes 12849152 | tf_op jit(solution)/shard_map/while/body/eval_jaxpr/rhd,khd->rhk/dot_general | solution.py:31
  93.7 2.4 %fusion.37 = f32[64,16]{0,1:T(8,128)S(1)} fusion(f32[16,2048,64]{1,2,0:T(8,128)S(1)} %get-tuple-element.367, f32[64,16]{0,1:T(8,128)S(1)} %get-tuple-element.368, pred[64,2048]{1,0:T(8,128)(4,1)S(1)} %broadcast_compare_fusion.2), kind=kLoop, calls=%fused_computation.4.clone.1 | loop fusion | flops 8387584 | bytes 8527872 | tf_op jit(solution)/shard_map/while/body/eval_jaxpr/reduce_sum | solution.py:36
  96.1 2.3 %fusion.38 = f32[64,16,64]{2,0,1:T(8,128)S(1)} fusion(bf16[2048,16,64]{0,2,1:T(8,128)(2,1)S(1)} %copy-done.1, f32[16,2048,64]{1,2,0:T(8,128)S(1)} %get-tuple-element.367, f32[64,16]{0,1:T(8,128)S(1)} %get-tuple-element.368, pred[64,2048]{1,0:T(8,128)(4,1)S(1)} %broadcast_compare_fusion.2, f32[64,16,64]{2,1,0:T(8,128)S(1)} %reshape.112, ...), kind=kOutput, calls=%fused_computation.13.clone.1 | convolution fusion | flops 277020672 | bytes 13250560 | tf_op jit(solution)/shard_map/while/body/eval_jaxpr/rhk,khd->rhd/dot_general | solution.py:37
  98.4 0.3 copy.42
  98.8 0.2 reshape.113
  99.1 0.6 collective-permute-start.2
  99.7 4.3 %collective-permute-start.3 = (f32[64,16]{0,1:T(8,128)S(1)}, f32[64,16]{0,1:T(8,128)S(1)}, u32[]{:S(2)}, u32[]{:S(2)}) collective-permute-start(f32[64,16]{0,1:T(8,128)S(1)} %get-tuple-element.372), channel_id=1, source_target_pairs={{0,4},{4,8},{8,12},{12,0},{1,5},{5,9},{9,13},{13,1},{2,6},{6,10},{... | collective-permute-start | bytes 12296 | tf_op jit(solution)/shard_map/while/body/eval_jaxpr/ppermute | solution.py:16
  103.9 5.6 %collective-permute-done.2 = f32[64,16]{0,1:T(8,128)S(1)} collective-permute-done((f32[64,16]{0,1:T(8,128)S(1)}, f32[64,16]{0,1:T(8,128)S(1)}, u32[]{:S(2)}, u32[]{:S(2)}) %collective-permute-start.2) | collective-permute-done | bytes 4128 | tf_op jit(solution)/shard_map/while/body/eval_jaxpr/ppermute | solution.py:16
  109.5 0.1 collective-permute-done.3
  109.6 0.1 copy.26
  109.7 0.2 div.11
  109.9 0.2 div.12
  110.1 5.7 %convolution_convert_fusion = bf16[64,4096]{1,0:T(8,128)(2,1)} fusion(bf16[1024,4096]{1,0:T(8,128)(2,1)} %param.12, f32[64,1024]{1,0:T(8,128)S(1)} %get-tuple-element.249, f32[64,1024]{1,0:T(8,128)S(1)} %div.12), kind=kOutput, calls=%fused_computation.24 | convolution fusion | flops 537264128 | bytes 9437184 | tf_op jit(solution)/shard_map/dot_general | solution.py:92
  115.8 19.2 %reduce-scatter.2.cloned.1.call-done = bf16[64,1024]{1,0:T(8,128)(2,1)} async-done(((bf16[64,4096]{1,0:T(8,128)(2,1)}), bf16[64,1024]{1,0:T(8,128)(2,1)}) %reduce-scatter.2.cloned.1.call-update) | async-done | bytes 131088 | tf_op jit(solution)/shard_map/reduce_scatter | solution.py:93
  (53 shorter events, 1.1 us)
Async XLA Ops:
  6.5 128.5 %reduce-scatter.2.cloned.1.call-start = ((), (), s32[]{:S(2)}) async-start(), calls=%async_computation.1 | async-start | bytes 655360 | tf_op jit(solution)/shard_map/reduce_scatter | solution.py:93
  7.5 13.1 %copy-start.3 = (s32[32]{0:T(128)S(1)}, s32[32]{0:T(128)}, u32[]{:S(2)}) copy-start(s32[32]{0:T(128)} %param.14) | copy-start | bytes 388
  7.5 13.3 %copy-start = (bf16[64,1024]{1,0:T(8,128)(2,1)S(1)}, bf16[64,1024]{1,0:T(8,128)(2,1)}, u32[]{:S(2)}) copy-start(bf16[64,1024]{1,0:T(8,128)(2,1)} %param.9) | copy-start | bytes 393220
  7.5 13.3 %copy-start.2 = (s32[256]{0:T(256)S(1)}, s32[256]{0:T(256)}, u32[]{:S(2)}) copy-start(s32[256]{0:T(256)} %param.15) | copy-start | bytes 3076
  21.6 6.3 %copy-start.1 = (bf16[2048,16,64]{0,2,1:T(8,128)(2,1)S(1)}, bf16[2048,16,64]{0,2,1:T(8,128)(2,1)}, u32[]{:S(2)}) copy-start(bf16[2048,16,64]{0,2,1:T(8,128)(2,1)} %get-tuple-element.413) | copy-start | bytes 12582916 | tf_op jit(solution)/shard_map/while
  30.7 14.6 %collective-permute-start.1 = (f32[64,1024]{1,0:T(8,128)S(1)}, f32[64,1024]{1,0:T(8,128)S(1)}, u32[]{:S(2)}, u32[]{:S(2)}) collective-permute-start(f32[64,1024]{1,0:T(8,128)S(1)} %reshape.113), channel_id=1, source_target_pairs={{0,4},{4,8},{8,12},{12,0},{1,5},{5,9},{9,13},{13,1},{2,6},{6,10},{... | collective-permute-start | bytes 786440 | tf_op jit(solution)/shard_map/while/body/eval_jaxpr/ppermute | solution.py:16
  33.8 11.5 %collective-permute-start = (bf16[64,1024]{1,0:T(8,128)(2,1)S(1)}, bf16[64,1024]{1,0:T(8,128)(2,1)S(1)}, u32[]{:S(2)}, u32[]{:S(2)}) collective-permute-start(bf16[64,1024]{1,0:T(8,128)(2,1)S(1)} %copy.49), channel_id=1, source_target_pairs={{0,4},{4,8},{8,12},{12,0},{1,5},{5,9},{9,13},{13,1},{2,6},{6,10},{... | collective-permute-start | bytes 393224 | tf_op jit(solution)/shard_map/while/body/eval_jaxpr/ppermute | solution.py:16
  35.4 9.8 %collective-permute-start.2 = (f32[64,16]{0,1:T(8,128)S(1)}, f32[64,16]{0,1:T(8,128)S(1)}, u32[]{:S(2)}, u32[]{:S(2)}) collective-permute-start(f32[64,16]{0,1:T(8,128)S(1)} %get-tuple-element.371), channel_id=1, source_target_pairs={{0,4},{4,8},{8,12},{12,0},{1,5},{5,9},{9,13},{13,1},{2,6},{6,10},{... | collective-permute-start | bytes 12296 | tf_op jit(solution)/shard_map/while/body/eval_jaxpr/ppermute | solution.py:16
  37.0 8.3 %collective-permute-start.3 = (f32[64,16]{0,1:T(8,128)S(1)}, f32[64,16]{0,1:T(8,128)S(1)}, u32[]{:S(2)}, u32[]{:S(2)}) collective-permute-start(f32[64,16]{0,1:T(8,128)S(1)} %get-tuple-element.372), channel_id=1, source_target_pairs={{0,4},{4,8},{8,12},{12,0},{1,5},{5,9},{9,13},{13,1},{2,6},{6,10},{... | collective-permute-start | bytes 12296 | tf_op jit(solution)/shard_map/while/body/eval_jaxpr/ppermute | solution.py:16
  46.0 6.3 %copy-start.1 = (bf16[2048,16,64]{0,2,1:T(8,128)(2,1)S(1)}, bf16[2048,16,64]{0,2,1:T(8,128)(2,1)}, u32[]{:S(2)}) copy-start(bf16[2048,16,64]{0,2,1:T(8,128)(2,1)} %get-tuple-element.413) | copy-start | bytes 12582916 | tf_op jit(solution)/shard_map/while
  55.2 12.5 %collective-permute-start.1 = (f32[64,1024]{1,0:T(8,128)S(1)}, f32[64,1024]{1,0:T(8,128)S(1)}, u32[]{:S(2)}, u32[]{:S(2)}) collective-permute-start(f32[64,1024]{1,0:T(8,128)S(1)} %reshape.113), channel_id=1, source_target_pairs={{0,4},{4,8},{8,12},{12,0},{1,5},{5,9},{9,13},{13,1},{2,6},{6,10},{... | collective-permute-start | bytes 786440 | tf_op jit(solution)/shard_map/while/body/eval_jaxpr/ppermute | solution.py:16
  55.2 12.4 %collective-permute-start = (bf16[64,1024]{1,0:T(8,128)(2,1)S(1)}, bf16[64,1024]{1,0:T(8,128)(2,1)S(1)}, u32[]{:S(2)}, u32[]{:S(2)}) collective-permute-start(bf16[64,1024]{1,0:T(8,128)(2,1)S(1)} %copy.49), channel_id=1, source_target_pairs={{0,4},{4,8},{8,12},{12,0},{1,5},{5,9},{9,13},{13,1},{2,6},{6,10},{... | collective-permute-start | bytes 393224 | tf_op jit(solution)/shard_map/while/body/eval_jaxpr/ppermute | solution.py:16
  56.5 11.1 %collective-permute-start.2 = (f32[64,16]{0,1:T(8,128)S(1)}, f32[64,16]{0,1:T(8,128)S(1)}, u32[]{:S(2)}, u32[]{:S(2)}) collective-permute-start(f32[64,16]{0,1:T(8,128)S(1)} %get-tuple-element.371), channel_id=1, source_target_pairs={{0,4},{4,8},{8,12},{12,0},{1,5},{5,9},{9,13},{13,1},{2,6},{6,10},{... | collective-permute-start | bytes 12296 | tf_op jit(solution)/shard_map/while/body/eval_jaxpr/ppermute | solution.py:16
  58.1 9.6 %collective-permute-start.3 = (f32[64,16]{0,1:T(8,128)S(1)}, f32[64,16]{0,1:T(8,128)S(1)}, u32[]{:S(2)}, u32[]{:S(2)}) collective-permute-start(f32[64,16]{0,1:T(8,128)S(1)} %get-tuple-element.372), channel_id=1, source_target_pairs={{0,4},{4,8},{8,12},{12,0},{1,5},{5,9},{9,13},{13,1},{2,6},{6,10},{... | collective-permute-start | bytes 12296 | tf_op jit(solution)/shard_map/while/body/eval_jaxpr/ppermute | solution.py:16
  68.3 6.3 %copy-start.1 = (bf16[2048,16,64]{0,2,1:T(8,128)(2,1)S(1)}, bf16[2048,16,64]{0,2,1:T(8,128)(2,1)}, u32[]{:S(2)}) copy-start(bf16[2048,16,64]{0,2,1:T(8,128)(2,1)} %get-tuple-element.413) | copy-start | bytes 12582916 | tf_op jit(solution)/shard_map/while
  77.5 11.6 %collective-permute-start.1 = (f32[64,1024]{1,0:T(8,128)S(1)}, f32[64,1024]{1,0:T(8,128)S(1)}, u32[]{:S(2)}, u32[]{:S(2)}) collective-permute-start(f32[64,1024]{1,0:T(8,128)S(1)} %reshape.113), channel_id=1, source_target_pairs={{0,4},{4,8},{8,12},{12,0},{1,5},{5,9},{9,13},{13,1},{2,6},{6,10},{... | collective-permute-start | bytes 786440 | tf_op jit(solution)/shard_map/while/body/eval_jaxpr/ppermute | solution.py:16
  77.6 11.5 %collective-permute-start = (bf16[64,1024]{1,0:T(8,128)(2,1)S(1)}, bf16[64,1024]{1,0:T(8,128)(2,1)S(1)}, u32[]{:S(2)}, u32[]{:S(2)}) collective-permute-start(bf16[64,1024]{1,0:T(8,128)(2,1)S(1)} %copy.49), channel_id=1, source_target_pairs={{0,4},{4,8},{8,12},{12,0},{1,5},{5,9},{9,13},{13,1},{2,6},{6,10},{... | collective-permute-start | bytes 393224 | tf_op jit(solution)/shard_map/while/body/eval_jaxpr/ppermute | solution.py:16
  77.6 11.4 %collective-permute-start.2 = (f32[64,16]{0,1:T(8,128)S(1)}, f32[64,16]{0,1:T(8,128)S(1)}, u32[]{:S(2)}, u32[]{:S(2)}) collective-permute-start(f32[64,16]{0,1:T(8,128)S(1)} %get-tuple-element.371), channel_id=1, source_target_pairs={{0,4},{4,8},{8,12},{12,0},{1,5},{5,9},{9,13},{13,1},{2,6},{6,10},{... | collective-permute-start | bytes 12296 | tf_op jit(solution)/shard_map/while/body/eval_jaxpr/ppermute | solution.py:16
  78.3 10.8 %collective-permute-start.3 = (f32[64,16]{0,1:T(8,128)S(1)}, f32[64,16]{0,1:T(8,128)S(1)}, u32[]{:S(2)}, u32[]{:S(2)}) collective-permute-start(f32[64,16]{0,1:T(8,128)S(1)} %get-tuple-element.372), channel_id=1, source_target_pairs={{0,4},{4,8},{8,12},{12,0},{1,5},{5,9},{9,13},{13,1},{2,6},{6,10},{... | collective-permute-start | bytes 12296 | tf_op jit(solution)/shard_map/while/body/eval_jaxpr/ppermute | solution.py:16
  89.7 6.3 %copy-start.1 = (bf16[2048,16,64]{0,2,1:T(8,128)(2,1)S(1)}, bf16[2048,16,64]{0,2,1:T(8,128)(2,1)}, u32[]{:S(2)}) copy-start(bf16[2048,16,64]{0,2,1:T(8,128)(2,1)} %get-tuple-element.413) | copy-start | bytes 12582916 | tf_op jit(solution)/shard_map/while
  98.9 10.7 %collective-permute-start.1 = (f32[64,1024]{1,0:T(8,128)S(1)}, f32[64,1024]{1,0:T(8,128)S(1)}, u32[]{:S(2)}, u32[]{:S(2)}) collective-permute-start(f32[64,1024]{1,0:T(8,128)S(1)} %reshape.113), channel_id=1, source_target_pairs={{0,4},{4,8},{8,12},{12,0},{1,5},{5,9},{9,13},{13,1},{2,6},{6,10},{... | collective-permute-start | bytes 786440 | tf_op jit(solution)/shard_map/while/body/eval_jaxpr/ppermute | solution.py:16
  99.0 10.6 %collective-permute-start = (bf16[64,1024]{1,0:T(8,128)(2,1)S(1)}, bf16[64,1024]{1,0:T(8,128)(2,1)S(1)}, u32[]{:S(2)}, u32[]{:S(2)}) collective-permute-start(bf16[64,1024]{1,0:T(8,128)(2,1)S(1)} %copy.49), channel_id=1, source_target_pairs={{0,4},{4,8},{8,12},{12,0},{1,5},{5,9},{9,13},{13,1},{2,6},{6,10},{... | collective-permute-start | bytes 393224 | tf_op jit(solution)/shard_map/while/body/eval_jaxpr/ppermute | solution.py:16
  99.1 10.4 %collective-permute-start.2 = (f32[64,16]{0,1:T(8,128)S(1)}, f32[64,16]{0,1:T(8,128)S(1)}, u32[]{:S(2)}, u32[]{:S(2)}) collective-permute-start(f32[64,16]{0,1:T(8,128)S(1)} %get-tuple-element.371), channel_id=1, source_target_pairs={{0,4},{4,8},{8,12},{12,0},{1,5},{5,9},{9,13},{13,1},{2,6},{6,10},{... | collective-permute-start | bytes 12296 | tf_op jit(solution)/shard_map/while/body/eval_jaxpr/ppermute | solution.py:16
  99.7 9.9 %collective-permute-start.3 = (f32[64,16]{0,1:T(8,128)S(1)}, f32[64,16]{0,1:T(8,128)S(1)}, u32[]{:S(2)}, u32[]{:S(2)}) collective-permute-start(f32[64,16]{0,1:T(8,128)S(1)} %get-tuple-element.372), channel_id=1, source_target_pairs={{0,4},{4,8},{8,12},{12,0},{1,5},{5,9},{9,13},{13,1},{2,6},{6,10},{... | collective-permute-start | bytes 12296 | tf_op jit(solution)/shard_map/while/body/eval_jaxpr/ppermute | solution.py:16
Sparse Core Ops, SparseCore 0:
  116.0 19.0 reduce-scatter.1
where the time goes:
time: 142 us
  waiting for transfers between devices  47.3 us (33%)
  matrix products  30.8 us (22%)
  starting transfers between devices  21.3 us (15%)
  local copies, waits for them, and re-layouts  18.2 us (13%)
  between operations  13.4 us (9%)
  other arithmetic  10.6 us (7%)
    ppermute x16, waiting for transfers between devices, shifted(): return lax.ppermute(value, axis, pairs)  28 us
    ppermute x16, starting transfers between devices, shifted(): return lax.ppermute(value, axis, pairs)  21.3 us
    reduce_scatter x1, waiting for transfers between devices, body(): lax.psum_scatter(projected.astype(jnp.bfloat16), ('heads', 'sub'), scatte...  19.2 us
    dot_general x4, matrix products, partial_state(): jnp.einsum('rhd,khd->rhk', query_heads, key_heads, preferred_element_type...  15.6 us
    unnamed x8, local copies, waits for them, and re-layouts  13.1 us
    reduce_sum x4, other arithmetic, partial_state(): totals = jnp.sum(terms, axis=2)  9.59 us
    dot_general x4, matrix products, partial_state(): jnp.einsum('rhk,khd->rhd', terms.astype(jnp.bfloat16), value_heads, prefe...  9.4 us
    dot_general x1, matrix products, body(): jnp.dot(attended, out_weight, preferred_element_type=jnp.float32)  5.75 us
  transfers between devices with their start and end apart: 17, of which 9 were waited for; matrix products, arithmetic and copies ran while one was open for 0% of the time, Pallas kernels for 0%

commit v1 on v0

v1 whole, which is shorter than its diff:
```python
import functools

import jax
import jax.numpy as jnp
from jax import lax
from jax.experimental import pallas as pl
from jax.experimental.pallas import tpu as pltpu
from jax.sharding import PartitionSpec as P

HEAD_DIM = 64
PLEN = 256
BEAMS = 16
CHUNK = 256
CHUNK_HEADS = CHUNK // HEAD_DIM
LANES = 128
FLOOR = -1e30
MESH = pl.DeviceIdType.MESH
f32 = jnp.float32
bf16 = jnp.bfloat16


def diagonal(wide):
    head = lax.broadcasted_iota(jnp.int32, (BEAMS, CHUNK), 1) // HEAD_DIM
    result = wide[:BEAMS]
    for h in range(1, CHUNK_HEADS):
        result = jnp.where(head == h, wide[h * BEAMS:(h + 1) * BEAMS], result)
    return result


def kernel(n, nx, chunks, *refs):
    q_ref, k_ref, v_ref, w_ref, counts, slot_of, beam_request, out_ref = refs[:8]
    refs = refs[8:]

    def take():
        nonlocal refs
        mine, refs = refs[:chunks], refs[chunks:]
        return mine

    qall, kbuf, vbuf, wbuf, obuf, stats, dest, lbuf, rbuf = [take() for _ in range(9)]
    (pacc, s1, r1, s2, r2, load_sem, ag_send, ag_recv, st_send, st_recv,
     rs_send, rs_recv, x_send, x_recv) = refs

    rows = q_ref.shape[0]
    slots = k_ref.shape[0] // PLEN
    width = out_ref.shape[1]
    me = lax.axis_index("blk")
    hx = lax.axis_index("heads")
    sub = lax.axis_index("sub")
    at_left, at_right = me == 0, me == n - 1

    loads = {}
    for g in range(chunks):
        cols = pl.ds(g * CHUNK, CHUNK)
        for i, (src, dst) in enumerate(
            ((k_ref.at[:, cols], kbuf[g]), (v_ref.at[:, cols], vbuf[g]), (w_ref.at[cols, :], wbuf[g]))
        ):
            loads[g, i] = pltpu.make_async_copy(src, dst, load_sem.at[g, i])
    own_q = [
        pltpu.make_async_copy(
            q_ref.at[:, pl.ds(g * CHUNK, CHUNK)], qall[g].at[pl.ds(me * rows, rows), :], load_sem.at[g, 3]
        )
        for g in range(chunks)
    ]
    for g in range(chunks):
        own_q[g].start()
    for i in (0, 1):
        loads[0, i].start()

    barrier = pltpu.get_barrier_semaphore()
    for d in range(1, n):
        pl.semaphore_signal(barrier, inc=1, device_id={"blk": lax.rem(me + d, n)}, device_id_type=MESH)
    for d in range(1, nx):
        pl.semaphore_signal(barrier, inc=1, device_id={"heads": lax.rem(hx + d, nx)}, device_id_type=MESH)
    pl.semaphore_signal(barrier, inc=1, device_id={"sub": 1 - sub}, device_id_type=MESH)

    def ag_copy(g, origin, way, first=False):
        src = qall[g].at[pl.ds(origin * rows, rows), :]
        return pltpu.make_async_remote_copy(
            src_ref=src,
            dst_ref=qall[g].at[pl.ds(origin * rows, rows), :],
            send_sem=ag_send.at[g, origin, way],
            recv_sem=ag_recv.at[g, origin],
            device_id={"blk": me + 1 if way == 0 else me - 1},
            device_id_type=MESH,
        )

    pl.semaphore_wait(barrier, (n - 1) + (nx - 1) + 1)
    for g in range(chunks):
        own_q[g].wait()

        @pl.when(jnp.logical_not(at_right))
        def _():
            ag_copy(g, me, 0).start()

        @pl.when(jnp.logical_not(at_left))
        def _():
            ag_copy(g, me, 1).start()

    for g in range(chunks):
        for i in (0, 1):
            if g:
                loads[g, i].start()
    for g in range(chunks):
        loads[g, 2].start()

    def ag_service(g):
        for d in range(1, n):
            @pl.when(me - d >= 0)
            def _():
                ag_copy(g, me - d, 0).wait_recv()

                @pl.when(jnp.logical_not(at_right))
                def _():
                    ag_copy(g, me - d, 0).start()

            @pl.when(me + d < n)
            def _():
                ag_copy(g, me + d, 1).wait_recv()

                @pl.when(jnp.logical_not(at_left))
                def _():
                    ag_copy(g, me + d, 1).start()

    slot_col = lax.broadcasted_iota(jnp.int32, (n * slots, LANES), 0)
    passage_col = jnp.zeros((n * slots, LANES), jnp.int32)
    for p in range(n * slots):
        passage_col = jnp.where(slot_col == slot_of[p], p, passage_col)
    owner_col = jnp.zeros((n * slots, LANES), jnp.int32)
    end = jnp.int32(0)
    for r in range(counts.shape[0]):
        end = end + counts[r]
        owner_col = owner_col + jnp.where(passage_col >= end, 1, 0)
    beams_col = jnp.zeros((n * slots, LANES), jnp.int32)
    for i in range(beam_request.shape[0] // BEAMS):
        beams_col = jnp.where(owner_col == beam_request[i * BEAMS], i, beams_col)

    def slot_row(col, s):
        return jnp.sum(jnp.where(slot_col == me * slots + s, col, 0), axis=0, keepdims=True)

    owners = [slot_row(owner_col, s) for s in range(slots)]
    lane_row = lax.broadcasted_iota(jnp.int32, (1, slots * BEAMS), 1)
    target = jnp.zeros((1, slots * BEAMS), jnp.int32)
    for s in range(slots):
        target = jnp.where(lane_row // BEAMS == s, slot_row(beams_col, s) * BEAMS, target)
    target = target + lane_row % BEAMS
    scatter = jnp.where(
        lax.broadcasted_iota(jnp.int32, (n * rows, slots * BEAMS), 0) == target, 1.0, 0.0
    ).astype(bf16)

    block_mask = jnp.where(
        lax.broadcasted_iota(jnp.int32, (CHUNK_HEADS * BEAMS, CHUNK), 0) // BEAMS
        == lax.broadcasted_iota(jnp.int32, (CHUNK_HEADS * BEAMS, CHUNK), 1) // HEAD_DIM,
        1.0, 0.0,
    ).astype(bf16)
    stat_lane = lax.broadcasted_iota(jnp.int32, (CHUNK_HEADS * BEAMS, LANES), 1)

    def st_copy(g, origin, other):
        return pltpu.make_async_remote_copy(
            src_ref=stats[g].at[origin],
            dst_ref=stats[g].at[origin],
            send_sem=st_send.at[g, other],
            recv_sem=st_recv.at[g, origin],
            device_id={"blk": other},
            device_id_type=MESH,
        )

    def compute(g):
        loads[g, 0].wait()
        loads[g, 1].wait()
        picked = lax.dot_general(
            scatter, qall[g][...], (((0,), (0,)), ((), ())), preferred_element_type=f32
        ).astype(bf16)
        lse_all = jnp.zeros((CHUNK_HEADS * BEAMS, LANES), f32)
        for s in range(slots):
            q = jnp.concatenate([picked[s * BEAMS:(s + 1) * BEAMS]] * CHUNK_HEADS, axis=0) * block_mask
            keys = kbuf[g][pl.ds(s * PLEN, PLEN), :]
            scores = lax.dot_general(q, keys, (((1,), (1,)), ((), ())), preferred_element_type=f32)
            top = jnp.max(scores, axis=1, keepdims=True)
            terms = jnp.exp(scores - top)
            total = jnp.sum(terms, axis=1, keepdims=True)
            summed = jnp.dot(terms.astype(bf16), vbuf[g][pl.ds(s * PLEN, PLEN), :], preferred_element_type=f32)
            obuf[g][pl.ds(s * BEAMS, BEAMS), :] = diagonal(summed * (1.0 / total))
            lse_all = jnp.where(stat_lane == s, top + jnp.log(total), lse_all)
        turned = jnp.concatenate([lse_all] * (LANES // (CHUNK_HEADS * BEAMS)), axis=0).T
        stats[g][me] = turned[:slots]
        for d in range(1, n):
            st_copy(g, me, lax.rem(me + d, n)).start()

    def finish(g):
        for d in range(1, n):
            other = lax.rem(me + d, n)
            st_copy(g, other, other).wait_recv()
        every = stats[g][...].reshape(n * slots, LANES)
        own = stats[g][me]
        factors = []
        for s in range(slots):
            part = jnp.where(owner_col == owners[s], every, FLOOR)
            top = jnp.max(part, axis=0, keepdims=True)
            total = jnp.sum(jnp.exp(part - top), axis=0, keepdims=True)
            factors.append(jnp.exp(own[s:s + 1] - top) / total)
        factors.append(jnp.zeros((LANES - slots, LANES), f32))
        factors = jnp.concatenate(factors, axis=0).T
        scaled = []
        for s in range(slots):
            column = jnp.broadcast_to(factors[:CHUNK_HEADS * BEAMS, s:s + 1], (CHUNK_HEADS * BEAMS, CHUNK))
            scaled.append((obuf[g][pl.ds(s * BEAMS, BEAMS), :] * diagonal(column)).astype(bf16))
        scaled = jnp.concatenate(scaled, axis=0)
        moved = jnp.dot(scatter, scaled, preferred_element_type=f32)
        dest[g][...] = moved.astype(bf16).reshape(n, rows, CHUNK)

    def rs_copy(g, to, way):
        land = lbuf[g] if way == 0 else rbuf[g]
        return pltpu.make_async_remote_copy(
            src_ref=dest[g].at[to],
            dst_ref=land.at[to],
            send_sem=rs_send.at[g, to, way],
            recv_sem=rs_recv.at[g, to, way],
            device_id={"blk": me + 1 if way == 0 else me - 1},
            device_id_type=MESH,
        )

    def add_arrived(g, to, way):
        rs_copy(g, to, way).wait_recv()
        land = lbuf[g] if way == 0 else rbuf[g]
        dest[g][to] = (dest[g][to].astype(f32) + land[to].astype(f32)).astype(bf16)

    def rs_hop(g):
        for d in range(n - 1, 0, -1):
            @pl.when(me + d < n)
            def _():
                @pl.when(jnp.logical_not(at_left))
                def _():
                    add_arrived(g, me + d, 0)

                rs_copy(g, me + d, 0).start()

            @pl.when(me - d >= 0)
            def _():
                @pl.when(jnp.logical_not(at_right))
                def _():
                    add_arrived(g, me - d, 1)

                rs_copy(g, me - d, 1).start()

    def x_copy(stage, index, other):
        return pltpu.make_async_remote_copy(
            src_ref=(s1 if stage == 0 else s2).at[other],
            dst_ref=(r1 if stage == 0 else r2).at[index],
            send_sem=x_send.at[stage, other],
            recv_sem=x_recv.at[stage, index],
            device_id={"sub": 1 - sub} if stage == 0 else {"heads": other},
            device_id_type=MESH,
        )

    def project(g):
        @pl.when(jnp.logical_not(at_left))
        def _():
            add_arrived(g, me, 0)

        @pl.when(jnp.logical_not(at_right))
        def _():
            add_arrived(g, me, 1)

        loads[g, 2].wait()
        attended = dest[g][me]
        last = g == chunks - 1

        def column(h, sb):
            block = h * 2 + sb
            part = jnp.dot(
                attended, wbuf[g][:, pl.ds(pl.multiple_of(block * width, LANES), width)],
                preferred_element_type=f32,
            )
            if g:
                part = part + pacc[block]
            return part

        for d in list(range(1, nx)) + [0]:
            other = lax.rem(hx + d, nx)
            part = column(other, 1 - sub)
            if last:
                s1[other] = part.astype(bf16)
                x_copy(0, other, other).start()
            else:
                pacc[other * 2 + 1 - sub] = part
        for d in list(range(1, nx)) + [0]:
            other = lax.rem(hx + d, nx)
            pacc[other * 2 + sub] = column(other, sub)

    for step in range(chunks + 3):
        if step < chunks:
            ag_service(step)
            compute(step)
        if 0 <= step - 1 < chunks:
            finish(step - 1)
        if 0 <= step - 2 < chunks:
            rs_hop(step - 2)
        if 0 <= step - 3 < chunks:
            project(step - 3)

    for d in range(1, nx):
        other = lax.rem(hx + d, nx)
        x_copy(0, other, other).wait_recv()
        s2[other] = (pacc[other * 2 + sub] + r1[other].astype(f32)).astype(bf16)
        x_copy(1, hx, other).start()
    x_copy(0, hx, hx).wait_recv()
    result = pacc[hx * 2 + sub] + r1[hx].astype(f32)
    for d in range(1, nx):
        other = lax.rem(hx + d, nx)
        x_copy(1, other, other).wait_recv()
        result = result + r2[other].astype(f32)
    out_ref[...] = result.astype(bf16)

    for g in range(chunks):
        for o in range(n):
            @pl.when(jnp.logical_and(o <= me, jnp.logical_not(at_right)))
            def _():
                ag_copy(g, o, 0).wait_send()

            @pl.when(jnp.logical_and(o >= me, jnp.logical_not(at_left)))
            def _():
                ag_copy(g, o, 1).wait_send()

            @pl.when(me < o)
            def _():
                rs_copy(g, o, 0).wait_send()

            @pl.when(me > o)
            def _():
                rs_copy(g, o, 1).wait_send()

        for d in range(1, n):
            st_copy(g, me, lax.rem(me + d, n)).wait_send()
    for h in range(nx):
        x_copy(0, h, h).wait_send()
    for d in range(1, nx):
        x_copy(1, hx, lax.rem(hx + d, nx)).wait_send()


def body(n, nx, queries, keys, values, out_weight, counts, slot_of, beam_request):
    rows, features = queries.shape
    chunks = features // CHUNK
    slots = keys.shape[0] // PLEN
    columns = out_weight.shape[1]
    width = columns // (nx * 2)
    dma = pltpu.SemaphoreType.DMA

    def per_chunk(shape, dtype):
        return [pltpu.VMEM(shape, dtype) for _ in range(chunks)]

    smem = pl.BlockSpec(memory_space=pltpu.SMEM)
    hbm = pl.BlockSpec(memory_space=pl.ANY)
    return pl.pallas_call(
        functools.partial(kernel, n, nx, chunks),
        out_shape=jax.ShapeDtypeStruct((rows, width), bf16),
        in_specs=[hbm] * 4 + [smem] * 3,
        out_specs=pl.BlockSpec(memory_space=pltpu.VMEM),
        scratch_shapes=(
            per_chunk((n * rows, CHUNK), bf16)
            + per_chunk((keys.shape[0], CHUNK), bf16)
            + per_chunk((keys.shape[0], CHUNK), bf16)
            + per_chunk((CHUNK, columns), bf16)
            + per_chunk((slots * BEAMS, CHUNK), f32)
            + per_chunk((n, slots, LANES), f32)
            + per_chunk((n, rows, CHUNK), bf16)
            + per_chunk((n, rows, CHUNK), bf16)
            + per_chunk((n, rows, CHUNK), bf16)
            + [
                pltpu.VMEM((nx * 2, rows, width), f32),
                pltpu.VMEM((nx, rows, width), bf16),
                pltpu.VMEM((nx, rows, width), bf16),
                pltpu.VMEM((nx, rows, width), bf16),
                pltpu.VMEM((nx, rows, width), bf16),
                dma((chunks, 4)),
                dma((chunks, n, 2)),
                dma((chunks, n)),
                dma((chunks, n)),
                dma((chunks, n)),
                dma((chunks, n, 2)),
                dma((chunks, n, 2)),
                dma((2, nx)),
                dma((2, nx)),
            ]
        ),
        compiler_params=pltpu.CompilerParams(
            collective_id=0, has_side_effects=True, vmem_limit_bytes=48 * 1024 * 1024
        ),
    )(queries, keys, values, out_weight, counts, slot_of, beam_request)


def solution(mesh):
    return jax.shard_map(
        functools.partial(body, mesh.shape["blk"], mesh.shape["heads"]),
        mesh=mesh,
        in_specs=(
            P(("groups", "blk"), ("heads", "sub")),
            P(("groups", "blk"), ("heads", "sub")),
            P(("groups", "blk"), ("heads", "sub")),
            P(("heads", "sub"), None),
            P("groups"),
            P("groups"),
            P("groups"),
        ),
        out_specs=P(("groups", "blk"), ("heads", "sub")),
        check_vma=False,
    )
```

time: 142 us -> 76.7 us (0.54)
  Pallas kernels: 0 us -> 70.7 us
  waiting for transfers between devices: 47.3 us -> 0 us
  matrix products: 30.8 us -> 0 us
  starting transfers between devices: 21.3 us -> 0 us
  between operations: 13.4 us -> 0.01 us
  local copies, waits for them, and re-layouts: 18.2 us -> 5.74 us
  other arithmetic: 10.6 us -> 0 us
    pallas_call x0 -> x1, Pallas kernels: none -> 70.7 us  [body(): pl.pallas_call(functools.partial(kernel, n, nx, chunks), out_shape=jax.Sh...]
    dot_general x9 -> x0, matrix products: 30.8 us -> none  [the longest x4 15.6 us: partial_state(): jnp.einsum('rhd,khd->rhk', query_heads, key_heads, preferred_element_type...]
    ppermute x16 -> x0, waiting for transfers between devices: 28 us -> none  [shifted(): return lax.ppermute(value, axis, pairs)]
    ppermute x16 -> x0, starting transfers between devices: 21.3 us -> none  [shifted(): return lax.ppermute(value, axis, pairs)]
    reduce_scatter x1 -> x0, waiting for transfers between devices: 19.2 us -> none  [body(): lax.psum_scatter(projected.astype(jnp.bfloat16), ('heads', 'sub'), scatte...]
    reduce_sum x6 -> x0, other arithmetic: 9.79 us -> none  [the longest x4 9.59 us: partial_state(): totals = jnp.sum(terms, axis=2)]
    unnamed x8 -> x11, local copies, waits for them, and re-layouts: 13.1 us -> 5.74 us
    reshape x12 -> x0, local copies, waits for them, and re-layouts: 1.95 us -> none  [the longest x4 0.71 us: partial_state(): query_heads = query_rows.reshape(row_count, heads_here, HEAD_DIM)]
  transfers between devices with their start and end apart: 17 -> 0, of which waited for: 9 -> 0; matrix products, arithmetic and copies ran while one was open for 0% -> 0% of each run, Pallas kernels for 0% -> 0%
where the time goes in v1:
time: 76.7 us; the launch traced here: 76.5 us
  Pallas kernels  70.7 us (92%)
  local copies, waits for them, and re-layouts  5.74 us (7%)
    pallas_call x1, Pallas kernels, body(): pl.pallas_call(functools.partial(kernel, n, nx, chunks), out_shape=jax.Sh...  70.7 us
    unnamed x11, local copies, waits for them, and re-layouts  5.74 us

profile of v1, /device:TPU:0, one launch (start us, length us, event | category | flops | bytes accessed | tf_op | source)
XLA Modules:
  0.0 76.5 jit_solution(171107482458392510)
XLA Ops:
  0.0 0.0 copy-start
  0.0 2.2 %copy-done = bf16[2048,1024]{1,0:T(8,128)(2,1)S(1)} copy-done((bf16[2048,1024]{1,0:T(8,128)(2,1)S(1)}, bf16[2048,1024]{1,0:T(8,128)(2,1)}, u32[]{:S(2)}) %copy-start) | copy-done | bytes 4194328
  2.2 0.0 copy-start.1
  2.2 0.9 %copy-done.1 = bf16[64,1024]{1,0:T(8,128)(2,1)S(1)} copy-done((bf16[64,1024]{1,0:T(8,128)(2,1)S(1)}, bf16[64,1024]{1,0:T(8,128)(2,1)}, u32[]{:S(2)}) %copy-start.1) | copy-done | bytes 131096
  3.1 0.0 copy-start.2
  3.1 0.7 copy-done.2
  3.8 0.0 copy-start.3
  3.8 0.7 copy-done.3
  4.4 0.0 copy-start.4
  4.4 0.7 copy-done.4
  5.1 70.7 %shard_map.73 = bf16[64,1024]{1,0:T(8,128)(2,1)S(1)} custom-call(bf16[64,1024]{1,0:T(8,128)(2,1)S(1)} %copy-done.1, bf16[2048,1024]{1,0:T(8,128)(2,1)S(1)} %copy-done, bf16[2048,1024]{1,0:T(8,128)(2,1)} %refs_2_.1, bf16[1024,4096]{1,0:T(8,128)(2,1)} %refs_3_.1, s32[16]{0:T(128)S(1)} %copy-done.3, s32[32]{0:T(128)S(1)} %copy-done.4, s32[256]{0:T(256)S(1)} %copy-done.2), custom_call_target="tpu_custom_call" | custom-call | tf_op jit(solution)/shard_map/pallas_call | solution.py:353
  75.8 0.7 copy.9
Async XLA Ops:
  0.0 2.2 %copy-start = (bf16[2048,1024]{1,0:T(8,128)(2,1)S(1)}, bf16[2048,1024]{1,0:T(8,128)(2,1)}, u32[]{:S(2)}) copy-start(bf16[2048,1024]{1,0:T(8,128)(2,1)} %refs_1_.1) | copy-start | bytes 12582916
  2.2 0.9 %copy-start.1 = (bf16[64,1024]{1,0:T(8,128)(2,1)S(1)}, bf16[64,1024]{1,0:T(8,128)(2,1)}, u32[]{:S(2)}) copy-start(bf16[64,1024]{1,0:T(8,128)(2,1)} %refs_0_.1) | copy-start | bytes 393220
  3.1 0.7 copy-start.2
  3.8 0.7 copy-start.3
  4.4 0.7 copy-start.4

commit v2 on v1

--- a/solution.py
+++ b/solution.py
@@ -36,7 +36,7 @@
         mine, refs = refs[:chunks], refs[chunks:]
         return mine
 
-    qall, kbuf, vbuf, wbuf, obuf, stats, dest, lbuf, rbuf = [take() for _ in range(9)]
+    qall, kbuf, vbuf, wbuf, obuf, stats, dest, land = [take() for _ in range(8)]
     (pacc, s1, r1, s2, r2, load_sem, ag_send, ag_recv, st_send, st_recv,
      rs_send, rs_recv, x_send, x_recv) = refs
 
@@ -46,7 +46,6 @@
     me = lax.axis_index("blk")
     hx = lax.axis_index("heads")
     sub = lax.axis_index("sub")
-    at_left, at_right = me == 0, me == n - 1
 
     loads = {}
     for g in range(chunks):
@@ -73,14 +72,14 @@
         pl.semaphore_signal(barrier, inc=1, device_id={"heads": lax.rem(hx + d, nx)}, device_id_type=MESH)
     pl.semaphore_signal(barrier, inc=1, device_id={"sub": 1 - sub}, device_id_type=MESH)
 
-    def ag_copy(g, origin, way, first=False):
-        src = qall[g].at[pl.ds(origin * rows, rows), :]
+    def ag_copy(g, origin, to):
+        rows_there = pl.ds(origin * rows, rows)
         return pltpu.make_async_remote_copy(
-            src_ref=src,
-            dst_ref=qall[g].at[pl.ds(origin * rows, rows), :],
-            send_sem=ag_send.at[g, origin, way],
+            src_ref=qall[g].at[rows_there, :],
+            dst_ref=qall[g].at[rows_there, :],
+            send_sem=ag_send.at[g, to],
             recv_sem=ag_recv.at[g, origin],
-            device_id={"blk": me + 1 if way == 0 else me - 1},
+            device_id={"blk": to},
             device_id_type=MESH,
         )
 
@@ -88,13 +87,8 @@
     for g in range(chunks):
         own_q[g].wait()
 
-        @pl.when(jnp.logical_not(at_right))
-        def _():
-            ag_copy(g, me, 0).start()
-
-        @pl.when(jnp.logical_not(at_left))
-        def _():
-            ag_copy(g, me, 1).start()
+        for d in range(1, n):
+            ag_copy(g, me, lax.rem(me + d, n)).start()
 
     for g in range(chunks):
         for i in (0, 1):
@@ -105,21 +99,8 @@
 
     def ag_service(g):
         for d in range(1, n):
-            @pl.when(me - d >= 0)
-            def _():
-                ag_copy(g, me - d, 0).wait_recv()
-
-                @pl.when(jnp.logical_not(at_right))
-                def _():
-                    ag_copy(g, me - d, 0).start()
-
-            @pl.when(me + d < n)
-            def _():
-                ag_copy(g, me + d, 1).wait_recv()
-
-                @pl.when(jnp.logical_not(at_left))
-                def _():
-                    ag_copy(g, me + d, 1).start()
+            other = lax.rem(me + d, n)
+            ag_copy(g, other, other).wait_recv()
 
     slot_col = lax.broadcasted_iota(jnp.int32, (n * slots, LANES), 0)
     passage_col = jnp.zeros((n * slots, LANES), jnp.int32)
@@ -208,39 +189,19 @@
         moved = jnp.dot(scatter, scaled, preferred_element_type=f32)
         dest[g][...] = moved.astype(bf16).reshape(n, rows, CHUNK)
 
-    def rs_copy(g, to, way):
-        land = lbuf[g] if way == 0 else rbuf[g]
+    def rs_copy(g, index, other):
         return pltpu.make_async_remote_copy(
-            src_ref=dest[g].at[to],
-            dst_ref=land.at[to],
-            send_sem=rs_send.at[g, to, way],
-            recv_sem=rs_recv.at[g, to, way],
-            device_id={"blk": me + 1 if way == 0 else me - 1},
+            src_ref=dest[g].at[other],
+            dst_ref=land[g].at[index],
+            send_sem=rs_send.at[g, other],
+            recv_sem=rs_recv.at[g, index],
+            device_id={"blk": other},
             device_id_type=MESH,
         )
 
-    def add_arrived(g, to, way):
-        rs_copy(g, to, way).wait_recv()
-        land = lbuf[g] if way == 0 else rbuf[g]
-        dest[g][to] = (dest[g][to].astype(f32) + land[to].astype(f32)).astype(bf16)
-
-    def rs_hop(g):
-        for d in range(n - 1, 0, -1):
-            @pl.when(me + d < n)
-            def _():
-                @pl.when(jnp.logical_not(at_left))
-                def _():
-                    add_arrived(g, me + d, 0)
-
-                rs_copy(g, me + d, 0).start()
-
-            @pl.when(me - d >= 0)
-            def _():
-                @pl.when(jnp.logical_not(at_right))
-                def _():
-                    add_arrived(g, me - d, 1)
-
-                rs_copy(g, me - d, 1).start()
+    def rs_start(g):
+        for d in range(1, n):
+            rs_copy(g, me, lax.rem(me + d, n)).start()
 
     def x_copy(stage, index, other):
         return pltpu.make_async_remote_copy(
@@ -253,16 +214,13 @@
         )
 
     def project(g):
-        @pl.when(jnp.logical_not(at_left))
-        def _():
-            add_arrived(g, me, 0)
-
-        @pl.when(jnp.logical_not(at_right))
-        def _():
-            add_arrived(g, me, 1)
-
+        attended = dest[g][me].astype(f32)
+        for d in range(1, n):
+            other = lax.rem(me + d, n)
+            rs_copy(g, other, other).wait_recv()
+            attended = attended + land[g][other].astype(f32)
+        attended = attended.astype(bf16)
         loads[g, 2].wait()
-        attended = dest[g][me]
         last = g == chunks - 1
 
         def column(h, sb):
@@ -293,8 +251,7 @@
             compute(step)
         if 0 <= step - 1 < chunks:
             finish(step - 1)
-        if 0 <= step - 2 < chunks:
-            rs_hop(step - 2)
+            rs_start(step - 1)
         if 0 <= step - 3 < chunks:
             project(step - 3)
 
@@ -312,25 +269,11 @@
     out_ref[...] = result.astype(bf16)
 
     for g in range(chunks):
-        for o in range(n):
-            @pl.when(jnp.logical_and(o <= me, jnp.logical_not(at_right)))
-            def _():
-                ag_copy(g, o, 0).wait_send()
-
-            @pl.when(jnp.logical_and(o >= me, jnp.logical_not(at_left)))
-            def _():
-                ag_copy(g, o, 1).wait_send()
-
-            @pl.when(me < o)
-            def _():
-                rs_copy(g, o, 0).wait_send()
-
-            @pl.when(me > o)
-            def _():
-                rs_copy(g, o, 1).wait_send()
-
-        for d in range(1, n):
-            st_copy(g, me, lax.rem(me + d, n)).wait_send()
+        for d in range(1, n):
+            other = lax.rem(me + d, n)
+            ag_copy(g, me, other).wait_send()
+            st_copy(g, me, other).wait_send()
+            rs_copy(g, me, other).wait_send()
     for h in range(nx):
         x_copy(0, h, h).wait_send()
     for d in range(1, nx):
@@ -364,7 +307,6 @@
             + per_chunk((n, slots, LANES), f32)
             + per_chunk((n, rows, CHUNK), bf16)
             + per_chunk((n, rows, CHUNK), bf16)
-            + per_chunk((n, rows, CHUNK), bf16)
             + [
                 pltpu.VMEM((nx * 2, rows, width), f32),
                 pltpu.VMEM((nx, rows, width), bf16),
@@ -372,18 +314,18 @@
                 pltpu.VMEM((nx, rows, width), bf16),
                 pltpu.VMEM((nx, rows, width), bf16),
                 dma((chunks, 4)),
-                dma((chunks, n, 2)),
-                dma((chunks, n)),
-                dma((chunks, n)),
-                dma((chunks, n)),
-                dma((chunks, n, 2)),
-                dma((chunks, n, 2)),
+                dma((chunks, n)),
+                dma((chunks, n)),
+                dma((chunks, n)),
+                dma((chunks, n)),
+                dma((chunks, n)),
+                dma((chunks, n)),
                 dma((2, nx)),
                 dma((2, nx)),
             ]
         ),
         compiler_params=pltpu.CompilerParams(
-            collective_id=0, has_side_effects=True, vmem_limit_bytes=48 * 1024 * 1024
+            collective_id=0, has_side_effects=True, vmem_limit_bytes=60 * 1024 * 1024
         ),
     )(queries, keys, values, out_weight, counts, slot_of, beam_request)
 

time: 76.7 us -> 43.4 us (0.57)
  Pallas kernels: 70.7 us -> 41.6 us
  local copies, waits for them, and re-layouts: 5.74 us -> 1.57 us
    pallas_call x1, Pallas kernels: 70.7 us -> 41.6 us  [body(): pl.pallas_call(functools.partial(kernel, n, nx, chunks), out_shape=jax.Sh...]
    unnamed x11 -> x1, local copies, waits for them, and re-layouts: 5.74 us -> 1.57 us
where the time goes in v2:
time: 43.4 us; the launch traced here: 43.2 us
  Pallas kernels  41.6 us (96%)
  local copies, waits for them, and re-layouts  1.57 us (4%)
    pallas_call x1, Pallas kernels, body(): pl.pallas_call(functools.partial(kernel, n, nx, chunks), out_shape=jax.Sh...  41.6 us
    unnamed x1, local copies, waits for them, and re-layouts  1.57 us

profile of v2, /device:TPU:0, one launch (start us, length us, event | category | flops | bytes accessed | tf_op | source)
XLA Modules:
  0.0 43.2 jit_solution(1922499644856347309)
XLA Ops:
  0.0 41.6 %shard_map.73 = bf16[64,1024]{1,0:T(8,128)(2,1)} custom-call(bf16[64,1024]{1,0:T(8,128)(2,1)} %refs_0_.1, bf16[2048,1024]{1,0:T(8,128)(2,1)} %refs_1_.1, bf16[2048,1024]{1,0:T(8,128)(2,1)} %refs_2_.1, bf16[1024,4096]{1,0:T(8,128)(2,1)} %refs_3_.1, s32[16]{0:T(128)} %refs_4_.1, s32[32]{0:T(128)} %refs_5_.1, s32[256]{0:T(256)} %refs_6_.1), custom_call_target="tpu_custom_call" | custom-call | tf_op jit(solution)/shard_map/pallas_call | solution.py:296
  41.6 1.6 %copy.9 = bf16[64,1024]{1,0:T(8,128)(2,1)} copy(bf16[64,1024]{1,0:T(8,128)(2,1)} %shard_map.73) | data formatting | bytes 262144

commit v3 on v2

--- a/solution.py
+++ b/solution.py
@@ -245,15 +245,15 @@
             other = lax.rem(hx + d, nx)
             pacc[other * 2 + sub] = column(other, sub)
 
-    for step in range(chunks + 3):
+    for step in range(chunks + 4):
         if step < chunks:
             ag_service(step)
             compute(step)
         if 0 <= step - 1 < chunks:
             finish(step - 1)
             rs_start(step - 1)
-        if 0 <= step - 3 < chunks:
-            project(step - 3)
+        if 0 <= step - 4 < chunks:
+            project(step - 4)
 
     for d in range(1, nx):
         other = lax.rem(hx + d, nx)

time: 43.4 us -> 43.4 us (level)
  no operation moved by 1% of the time
where the time goes in v3:
time: 43.4 us; the launch traced here: 43.3 us
  Pallas kernels  41.7 us (96%)
  local copies, waits for them, and re-layouts  1.57 us (4%)
    pallas_call x1, Pallas kernels, body(): pl.pallas_call(functools.partial(kernel, n, nx, chunks), out_shape=jax.Sh...  41.7 us
    unnamed x1, local copies, waits for them, and re-layouts  1.57 us

profile of v3, /device:TPU:0, one launch (start us, length us, event | category | flops | bytes accessed | tf_op | source)
XLA Modules:
  0.0 43.3 jit_solution(3802634128421327061)
XLA Ops:
  0.0 41.7 %shard_map.73 = bf16[64,1024]{1,0:T(8,128)(2,1)} custom-call(bf16[64,1024]{1,0:T(8,128)(2,1)} %refs_0_.1, bf16[2048,1024]{1,0:T(8,128)(2,1)} %refs_1_.1, bf16[2048,1024]{1,0:T(8,128)(2,1)} %refs_2_.1, bf16[1024,4096]{1,0:T(8,128)(2,1)} %refs_3_.1, s32[16]{0:T(128)} %refs_4_.1, s32[32]{0:T(128)} %refs_5_.1, s32[256]{0:T(256)} %refs_6_.1), custom_call_target="tpu_custom_call" | custom-call | tf_op jit(solution)/shard_map/pallas_call | solution.py:296
  41.7 1.6 %copy.9 = bf16[64,1024]{1,0:T(8,128)(2,1)} copy(bf16[64,1024]{1,0:T(8,128)(2,1)} %shard_map.73) | data formatting | bytes 262144
